TPU v7x, 32 devices: a whole 2x2x4 slice. The times are simulated.
32 devices in a mesh: lat: 8 (over y, x, core), lon: 4 (over z).
Axes of the slice: x: 2, y: 2, z: 4, core: 2. Of those that a mesh axis runs over, the one named last changes fastest.
Arguments:
- lower: float32 [32, 524288], P(None, ('lat', 'lon')), may hold values from 0.05 to 4
- upper: float32 [32, 524288], P(None, ('lat', 'lon')), may hold values from 0.05 to 4
- old_temp: float32 [32, 524288], P(None, ('lat', 'lon')), may hold values from -6 to 6
- atm_area: float32 [524288], P(('lat', 'lon')), may hold values from 0.5 to 2
- pair_count: int32 [32, 10], P(('lat', 'lon')), may hold values from 0 to 4096, as said below
- cell_column: int32 [32, 10, 4096], P(('lat', 'lon')), may hold values from 0 to 16383
- exchange_cell_weight: float32 [32, 10, 4096], P(('lat', 'lon')), may hold values from 0.1 to 1
- cell_coef: float32 [32, 10, 4096], P(('lat', 'lon')), may hold values from 0.3 to 3
- cell_ocean: int32 [32, 10, 4096], P(('lat', 'lon')), may hold values from 0 to 16383
- surface_temp: float32 [524288], P(('lat', 'lon')), may hold values from -6 to 6
- extra_warming: float32 [524288], P(('lat', 'lon')), may hold values from -6 to 6
- response: float32 [524288], P(('lat', 'lon')), may hold values from 0.1 to 1
- sea_mask: int32 [524288], P(('lat', 'lon')), may hold values 0 or 1
- ocean_area: float32 [524288], P(('lat', 'lon')), may hold values from 0.5 to 2
Outputs:
- level_warmth_new: float32 [32, 524288], P(None, ('lat', 'lon'))
- fresh_seawater_warmth: float32 [524288], P(('lat', 'lon'))
Inputs may be any that keep to these rules, and one draw needn't show every extreme that they name: pair_count is 0 for every offset whose partner does not exist and 1 or more for every other; for every atmosphere owner the offset 4 pair (its own block) has all 4096 slots live.
All inputs are finite; a program needn't handle non-finite values. No bound on the sum of `sea_mask` on one device may be relied on, other than what follows from the above.
Results may differ from a plain program's by a relative error of at most 0.00002.
Values sent between devices are 32-bit elements; how exact they have to be, the bound alone decides.
A program may use at most 128 MiB of HBM per device.

v0:
```python
import functools

import jax
import jax.numpy as jnp
from jax import lax
from jax.experimental import pallas as pl
from jax.experimental.pallas import tpu as pltpu
from jax.sharding import PartitionSpec as P

LANES = 128
SUB = 8
LOCAL = 4
F32 = jnp.float32
BF16 = jnp.bfloat16


def parts_of(value):
    high = value.astype(BF16)
    low = (value - high.astype(F32)).astype(BF16)
    return high, low


def offset_of(k, half):
    last = k // 9
    r = (k // 3 - 1) * (1 - last)
    c = (k % 3 - 1) * (1 - last) + half * last
    return r, c


def kernel(
    n_lat,
    n_lon,
    count_ref,
    *refs,
):
    sources, (level_hbm, fresh_ref), refs = refs[:13], refs[13:15], refs[15:]
    (
        ocean_ref,
        surface_ref,
        warming_ref,
        response_ref,
        mask_ref,
        column_ref,
        weight_ref,
        coef_ref,
        atm_area_ref,
        ocean_area_ref,
        lower,
        upper,
        temp,
    ) = refs[:13]
    (
        e_all,
        g_all,
        level,
        ocean_table,
        atm_table,
        f_low,
        picked,
        arrived,
        weighted,
        returned,
        atm_sum,
        ocean_sum,
        load_sem,
        store_sem,
        out_sem,
        in_sem,
        back_out_sem,
        back_in_sem,
    ) = refs[13:]
    offsets, blocks, _ = column_ref.shape
    rows = f_low.shape[0]
    levels = e_all.shape[0]
    pieces = blocks // SUB
    i = lax.axis_index("lat")
    j = lax.axis_index("lon")

    def partner(k, sign):
        r, c = offset_of(k, n_lon // 2)
        row = i + sign * r
        col = (j + sign * c + n_lon) % n_lon
        there = (row >= 0) & (row < n_lat) & ((k < 9) | (row == n_lat - 1))
        return row, col, there

    def order(t):
        return t + (t + 4) // 8 - (t // 9) * 6

    loads = [
        pltpu.make_async_copy(source, dest, load_sem.at[n])
        for n, (source, dest) in enumerate(zip(sources, refs[:13]))
    ]
    for load in loads:
        load.start()

    barrier = pltpu.get_barrier_semaphore()

    @pl.loop(0, offsets)
    def _(k):
        row, col, there = partner(k, 1)

        @pl.when(there & (k != LOCAL))
        def _():
            pl.semaphore_signal(
                barrier, inc=1, device_id=(row, col), device_id_type=pl.DeviceIdType.MESH
            )

    def send(k):
        row, col, there = partner(k, -1)
        copy = pltpu.make_async_remote_copy(
            src_ref=picked.at[k],
            dst_ref=arrived.at[k],
            send_sem=out_sem.at[k],
            recv_sem=in_sem.at[k],
            device_id=(row, col),
            device_id_type=pl.DeviceIdType.MESH,
        )
        return copy, there

    def send_back(k):
        row, col, there = partner(k, 1)
        copy = pltpu.make_async_remote_copy(
            src_ref=weighted.at[k],
            dst_ref=returned.at[k],
            send_sem=back_out_sem.at[k],
            recv_sem=back_in_sem.at[k],
            device_id=(row, col),
            device_id_type=pl.DeviceIdType.MESH,
        )
        return copy, there

    wide = 2 * LANES
    lane_places = lax.broadcasted_iota(jnp.int32, (LANES, wide), 0).astype(F32).astype(BF16)
    row_places = lax.broadcasted_iota(jnp.int32, (rows, wide), 0).astype(F32).astype(BF16)
    sub_places = lax.broadcasted_iota(jnp.int32, (SUB, wide), 0)
    sublane = lax.broadcasted_iota(jnp.int32, (SUB, LANES), 0)

    def split(index):
        return lax.shift_right_logical(index, 7), index & (LANES - 1)

    def pair(value, b):
        return jnp.concatenate([value[b : b + 1], value[b + 1 : b + 2]], axis=1)

    def spread(value, count):
        value = jnp.broadcast_to(value, (2 * SUB, wide)).astype(BF16)
        return jnp.concatenate([value] * (count // (2 * SUB)), axis=0)

    def one_hot(places, index):
        return jnp.where(
            places == spread(index, places.shape[0]), BF16(1.0), BF16(0.0)
        )

    def gather(table, index):
        high, low = split(index)
        low = low.astype(F32)
        first = jnp.zeros((SUB, LANES), F32)
        second = jnp.zeros((SUB, LANES), F32)
        for b in range(0, SUB, 2):
            hot = one_hot(lane_places, pair(low, b))
            found = jnp.dot(
                table[...], jnp.concatenate([hot, hot], axis=0), preferred_element_type=F32
            )
            at = jnp.broadcast_to(pair(high, b), (SUB, wide))
            on = {}
            bit = SUB
            while bit < rows:
                on[bit] = (at & bit) != 0
                bit *= 2
            own = sub_places == (at & (SUB - 1))

            def choose(start, count):
                if count == SUB:
                    return found[start : start + SUB]
                half = count // 2
                below = choose(start, half)
                above = choose(start + half, half)
                return jnp.where(on[half], above, below)

            def pick(start):
                value = jnp.where(own, choose(start, rows), 0.0)
                return jnp.sum(value, axis=0, keepdims=True)

            one, two = pick(0), pick(rows)
            for half in range(2):
                mine = sublane == b + half
                part = slice(half * LANES, (half + 1) * LANES)
                first = jnp.where(mine, one[:, part], first)
                second = jnp.where(mine, two[:, part], second)
        return first, second

    def scatter(index, value):
        high, low = split(index)
        high = high.astype(F32)
        low = low.astype(F32)
        big, small = parts_of(value)
        big = big.astype(F32)
        small = small.astype(F32)
        hots, spreads = [], []
        for b in range(0, SUB, 2):
            mine = lane_places == spread(pair(low, b), LANES)
            values = [
                jnp.where(mine, spread(pair(part, b), LANES), BF16(0.0)) for part in (big, small)
            ]
            hots.append(one_hot(row_places, pair(high, b)))
            spreads.append(jnp.concatenate(values, axis=0))
        return lax.dot_general(
            jnp.concatenate(hots, axis=1),
            jnp.concatenate(spreads, axis=1),
            (((1,), (1,)), ((), ())),
            preferred_element_type=F32,
        )

    def span(n):
        return pl.ds(n * SUB, SUB)

    def fill(table, first, second):
        for at, value in ((0, first), (rows, second)):
            high, low = parts_of(value)
            table[at : at + rows, :LANES] = high
            table[at : at + rows, LANES:] = low

    for load in loads[:5]:
        load.wait()
    gsea = response_ref[...] * mask_ref[...].astype(F32)
    fill(ocean_table, surface_ref[...] + gsea * warming_ref[...], gsea)

    expected = jnp.int32(0)
    for k in range(offsets):
        if k != LOCAL:
            expected = expected + partner(jnp.int32(k), -1)[2].astype(jnp.int32)
    pl.semaphore_wait(barrier, expected)

    @pl.loop(0, offsets)
    def _(t):
        k = order(t)
        copy, there = send(k)

        @pl.when(there)
        def _():
            for n in range(pieces):
                first, second = gather(ocean_table, ocean_ref[k, span(n), :])
                picked[k, 0, span(n), :] = first
                picked[k, 1, span(n), :] = second

        @pl.when(there & (k != LOCAL))
        def _():
            copy.start()

    arrived[LOCAL] = picked[LOCAL]

    for load in loads[5:]:
        load.wait()

    group = min(rows, 64)

    def at_level(k, base):
        first = (k // SUB) * rows * SUB + (k % SUB)
        return pl.ds(first + base * SUB, group, stride=SUB)

    @pl.loop(0, rows // group)
    def _(b):
        base = pl.multiple_of(b * group, group)
        e = jnp.zeros((group, LANES), F32)
        g = jnp.zeros((group, LANES), F32)
        for k in range(levels - 1, -1, -1):
            low = lower[at_level(k, base), :]
            up = upper[at_level(k, base), :]
            rhs = temp[at_level(k, base), :]
            inverse = 1.0 / (1.0 + low + up - up * g)
            e = (rhs + up * e) * inverse
            g = low * inverse
            e_all[k, pl.ds(base, group), :] = e
            if k:
                g_all[k, pl.ds(base, group), :] = g
        f_low[pl.ds(base, group), :] = inverse

    fill(atm_table, e_all[0], f_low[...])
    atm_sum[...] = jnp.zeros_like(atm_sum)

    @pl.loop(0, offsets)
    def _(t):
        k = order(t)
        _, _, there = partner(k, 1)
        incoming, _ = send(k)
        copy, _ = send_back(k)

        @pl.when(there & (k != LOCAL))
        def _():
            incoming.wait_recv()

        @pl.when(there)
        def _():
            live_slots = count_ref[0, k]

            total = atm_sum[...]
            for n in range(pieces):
                index = column_ref[k, span(n), :]
                e, f = gather(atm_table, index)
                coef = coef_ref[k, span(n), :]
                target = arrived[k, 0, span(n), :]
                response = arrived[k, 1, span(n), :]
                flux = coef * (target - e) / (1.0 + coef * (response + f))
                lane = lax.broadcasted_iota(jnp.int32, (SUB, LANES), 1)
                slot = (n * SUB + sublane) * LANES + lane
                value = jnp.where(slot < live_slots, weight_ref[k, span(n), :] * flux, 0.0)
                weighted[k, span(n), :] = value
                total = total + scatter(index, value)
            atm_sum[...] = total

        @pl.when(there & (k != LOCAL))
        def _():
            copy.start()

    returned[LOCAL] = weighted[LOCAL]

    @pl.loop(0, rows // group)
    def _(b):
        base = pl.multiple_of(b * group, group)
        here = pl.ds(base, group)
        flux = (atm_sum[here, :LANES] + atm_sum[here, LANES:]) / atm_area_ref[here, :]
        value = e_all[0, here, :] + f_low[here, :] * flux
        level[at_level(0, base), :] = value
        for k in range(1, levels):
            value = e_all[k, here, :] + g_all[k, here, :] * value
            level[at_level(k, base), :] = value

    store = pltpu.make_async_copy(level, level_hbm, store_sem)
    store.start()
    ocean_sum[...] = jnp.zeros_like(ocean_sum)

    @pl.loop(0, offsets)
    def _(t):
        k = order(t)
        _, _, there = partner(k, -1)
        incoming, _ = send_back(k)

        @pl.when(there & (k != LOCAL))
        def _():
            incoming.wait_recv()

        @pl.when(there)
        def _():
            total = ocean_sum[...]
            for n in range(pieces):
                total = total + scatter(ocean_ref[k, span(n), :], returned[k, span(n), :])
            ocean_sum[...] = total

    ocean_flux = (ocean_sum[:, :LANES] + ocean_sum[:, LANES:]) / ocean_area_ref[...]
    gsea = response_ref[...] * mask_ref[...].astype(F32)
    fresh_ref[...] = surface_ref[...] + gsea * (warming_ref[...] - ocean_flux)

    @pl.loop(0, offsets)
    def _(k):
        forth, there = send(k)

        @pl.when(there & (k != LOCAL))
        def _():
            forth.wait_send()

        back, there = send_back(k)

        @pl.when(there & (k != LOCAL))
        def _():
            back.wait_send()

    store.wait()


def on_device(
    n_lat,
    n_lon,
    lower,
    upper,
    old_temp,
    atm_area,
    pair_count,
    cell_column,
    exchange_cell_weight,
    cell_coef,
    cell_ocean,
    surface_temp,
    extra_warming,
    response,
    sea_mask,
    ocean_area,
):
    levels, ncols = lower.shape
    rows = ncols // LANES
    _, offsets, slots = cell_column.shape

    def tiles(array):
        array = array.reshape(levels // SUB, SUB, rows, LANES)
        return array.transpose(0, 2, 1, 3).reshape(levels * rows, LANES)

    def square(array):
        return array.reshape(-1, LANES)

    def cells(array):
        return array.reshape(offsets, slots // LANES, LANES)

    operands = [cells(cell_ocean)]
    operands += [square(a) for a in (surface_temp, extra_warming, response, sea_mask)]
    operands += [cells(a) for a in (cell_column, exchange_cell_weight, cell_coef)]
    operands += [square(a) for a in (atm_area, ocean_area)]
    operands += [tiles(a) for a in (lower, upper, old_temp)]
    vmem = pl.BlockSpec(memory_space=pltpu.VMEM)
    smem = pl.BlockSpec(memory_space=pltpu.SMEM)
    hbm = pl.BlockSpec(memory_space=pl.ANY)
    flat = pltpu.VMEM((levels * rows, LANES), F32)
    deep = pltpu.VMEM((levels, rows, LANES), F32)
    table = pltpu.VMEM((2 * rows, 2 * LANES), BF16)
    states = pltpu.VMEM((offsets, 2, slots // LANES, LANES), F32)
    fluxes = pltpu.VMEM((offsets, slots // LANES, LANES), F32)
    total = pltpu.VMEM((rows, 2 * LANES), F32)
    sem = pltpu.SemaphoreType.DMA((offsets,))
    level, fresh = pl.pallas_call(
        functools.partial(kernel, n_lat, n_lon),
        out_shape=(
            jax.ShapeDtypeStruct((levels * rows, LANES), F32),
            jax.ShapeDtypeStruct((rows, LANES), F32),
        ),
        in_specs=[smem] + [hbm] * len(operands),
        out_specs=(hbm, vmem),
        scratch_shapes=[pltpu.VMEM(a.shape, a.dtype) for a in operands]
        + [
            deep,
            deep,
            flat,
            table,
            table,
            pltpu.VMEM((rows, LANES), F32),
            states,
            states,
            fluxes,
            fluxes,
            total,
            total,
            pltpu.SemaphoreType.DMA((len(operands),)),
            pltpu.SemaphoreType.DMA,
            sem,
            sem,
            sem,
            sem,
        ],
        compiler_params=pltpu.CompilerParams(
            collective_id=0, has_side_effects=True, vmem_limit_bytes=60 * 1024 * 1024
        ),
    )(pair_count, *operands)
    level = level.reshape(levels // SUB, rows, SUB, LANES).transpose(0, 2, 1, 3)
    return level.reshape(levels, ncols), fresh.reshape(-1)


def solution(mesh):
    owners = ("lat", "lon")
    level = P(None, owners)
    single = P(owners)
    pairs = P(owners, None)
    cells = P(owners, None, None)
    return jax.shard_map(
        functools.partial(on_device, mesh.shape["lat"], mesh.shape["lon"]),
        mesh=mesh,
        in_specs=(level, level, level, single, pairs, cells, cells, cells, cells)
        + (single,) * 5,
        out_specs=(level, single),
        check_vma=False,
    )
```

profile of v0, /device:TPU:1, one launch (start us, length us, event | category | flops | bytes accessed | tf_op | source)
XLA Modules:
  0.0 46.6 jit_solution(17296982852112776628)
XLA Ops:
  0.6 42.2 %shard_map.149 = (f32[4096,128]{1,0:T(8,128)}, f32[128,128]{1,0:T(8,128)}) custom-call(s32[1,10]{1,0:T(1,128)} %count_ref.1, s32[10,32,128]{2,1,0:T(8,128)} %bitcast.35, f32[128,128]{1,0:T(8,128)} %bitcast.40, f32[128,128]{1,0:T(8,128)} %bitcast.41, f32[128,128]{1,0:T(8,128)} %bitcast.42, s32[128,128]{1,0:T(8,128)} %bitcast.43, s32[10,32,128]{2,1,0:T(8,128)} %bitcast.36, ...), custom_call_target="tpu_custom_call" | custom-call | tf_op jit(solution)/shard_map/pallas_call | solution.py:416
  42.8 0.0 copy-start
  42.9 3.1 %copy.18 = f32[32,16384]{1,0:T(8,128)} copy(f32[32,16384]{1,0:T(8,128)} %bitcast.31) | data formatting | bytes 4194304
  45.9 0.0 copy-done
  45.9 0.6 %copy.19 = f32[16384]{0:T(1024)} copy(f32[16384]{0:T(1024)S(1)} %bitcast.39) | data formatting | bytes 131072
Async XLA Ops:
  42.8 3.1 %copy-start = (f32[128,128]{1,0:T(8,128)S(1)}, f32[128,128]{1,0:T(8,128)}, u32[]{:S(2)}) copy-start(f32[128,128]{1,0:T(8,128)} %get-tuple-element.5) | copy-start | bytes 196612
where the time goes:
time: 46.7 us; the launch traced here: 46.6 us
  Pallas kernels  42.2 us (90%)
  local copies, waits for them, and re-layouts  3.72 us (8%)
  between operations  0.65 us (1%)
    pallas_call x1, Pallas kernels, on_device(): pl.pallas_call(functools.partial(kernel, n_lat, n_lon), out_shape=(jax.Sh...  42.2 us
    unnamed x4, local copies, waits for them, and re-layouts  3.72 us

commit v1 on v0

--- a/solution.py
+++ b/solution.py
@@ -27,108 +27,24 @@
     return r, c
 
 
-def kernel(
-    n_lat,
-    n_lon,
-    count_ref,
-    *refs,
-):
-    sources, (level_hbm, fresh_ref), refs = refs[:13], refs[13:15], refs[15:]
-    (
-        ocean_ref,
-        surface_ref,
-        warming_ref,
-        response_ref,
-        mask_ref,
-        column_ref,
-        weight_ref,
-        coef_ref,
-        atm_area_ref,
-        ocean_area_ref,
-        lower,
-        upper,
-        temp,
-    ) = refs[:13]
-    (
-        e_all,
-        g_all,
-        level,
-        ocean_table,
-        atm_table,
-        f_low,
-        picked,
-        arrived,
-        weighted,
-        returned,
-        atm_sum,
-        ocean_sum,
-        load_sem,
-        store_sem,
-        out_sem,
-        in_sem,
-        back_out_sem,
-        back_in_sem,
-    ) = refs[13:]
-    offsets, blocks, _ = column_ref.shape
-    rows = f_low.shape[0]
-    levels = e_all.shape[0]
-    pieces = blocks // SUB
-    i = lax.axis_index("lat")
-    j = lax.axis_index("lon")
-
-    def partner(k, sign):
-        r, c = offset_of(k, n_lon // 2)
-        row = i + sign * r
-        col = (j + sign * c + n_lon) % n_lon
-        there = (row >= 0) & (row < n_lat) & ((k < 9) | (row == n_lat - 1))
-        return row, col, there
-
-    def order(t):
-        return t + (t + 4) // 8 - (t // 9) * 6
-
-    loads = [
-        pltpu.make_async_copy(source, dest, load_sem.at[n])
-        for n, (source, dest) in enumerate(zip(sources, refs[:13]))
-    ]
-    for load in loads:
-        load.start()
-
-    barrier = pltpu.get_barrier_semaphore()
-
-    @pl.loop(0, offsets)
-    def _(k):
-        row, col, there = partner(k, 1)
-
-        @pl.when(there & (k != LOCAL))
-        def _():
-            pl.semaphore_signal(
-                barrier, inc=1, device_id=(row, col), device_id_type=pl.DeviceIdType.MESH
-            )
-
-    def send(k):
-        row, col, there = partner(k, -1)
-        copy = pltpu.make_async_remote_copy(
-            src_ref=picked.at[k],
-            dst_ref=arrived.at[k],
-            send_sem=out_sem.at[k],
-            recv_sem=in_sem.at[k],
-            device_id=(row, col),
-            device_id_type=pl.DeviceIdType.MESH,
-        )
-        return copy, there
-
-    def send_back(k):
-        row, col, there = partner(k, 1)
-        copy = pltpu.make_async_remote_copy(
-            src_ref=weighted.at[k],
-            dst_ref=returned.at[k],
-            send_sem=back_out_sem.at[k],
-            recv_sem=back_in_sem.at[k],
-            device_id=(row, col),
-            device_id_type=pl.DeviceIdType.MESH,
-        )
-        return copy, there
-
+def partner_of(n_lat, n_lon, k, sign):
+    r, c = offset_of(k, n_lon // 2)
+    row = lax.axis_index("lat") + sign * r
+    col = (lax.axis_index("lon") + sign * c + n_lon) % n_lon
+    there = (row >= 0) & (row < n_lat) & ((k < 9) | (row == n_lat - 1))
+    return row, col, there
+
+
+def order(t):
+    return t + (t + 4) // 8 - (t // 9) * 6
+
+
+def at_level(k, base, rows, group):
+    first = (k // SUB) * rows * SUB + (k % SUB)
+    return pl.ds(first + base * SUB, group, stride=SUB)
+
+
+def helpers(rows):
     wide = 2 * LANES
     lane_places = lax.broadcasted_iota(jnp.int32, (LANES, wide), 0).astype(F32).astype(BF16)
     row_places = lax.broadcasted_iota(jnp.int32, (rows, wide), 0).astype(F32).astype(BF16)
@@ -219,6 +135,102 @@
             table[at : at + rows, :LANES] = high
             table[at : at + rows, LANES:] = low
 
+
+    return sublane, gather, scatter, span, fill
+
+
+def kernel(
+    n_lat,
+    n_lon,
+    count_ref,
+    *refs,
+):
+    sources, outputs, refs = refs[:12], refs[12:16], refs[16:]
+    e_hbm, g_hbm, bottom_hbm, returned = outputs
+    (
+        ocean_ref,
+        surface_ref,
+        warming_ref,
+        response_ref,
+        mask_ref,
+        lower,
+        upper,
+        temp,
+        column_ref,
+        weight_ref,
+        coef_ref,
+        atm_area_ref,
+    ) = refs[:12]
+    (
+        e_all,
+        g_all,
+        bottom,
+        ocean_table,
+        atm_table,
+        f_low,
+        picked,
+        arrived,
+        weighted,
+        atm_sum,
+        load_sem,
+        store_sem,
+        own_sem,
+        out_sem,
+        in_sem,
+        back_out_sem,
+        back_in_sem,
+    ) = refs[12:]
+    offsets, blocks, _ = column_ref.shape
+    rows = f_low.shape[0]
+    levels = e_all.shape[0]
+    pieces = blocks // SUB
+    partner = functools.partial(partner_of, n_lat, n_lon)
+
+    loads = [
+        pltpu.make_async_copy(source, dest, load_sem.at[n])
+        for n, (source, dest) in enumerate(zip(sources, refs[:12]))
+    ]
+    for load in loads:
+        load.start()
+
+    barrier = pltpu.get_barrier_semaphore()
+
+    @pl.loop(0, offsets)
+    def _(k):
+        row, col, there = partner(k, 1)
+
+        @pl.when(there & (k != LOCAL))
+        def _():
+            pl.semaphore_signal(
+                barrier, inc=1, device_id=(row, col), device_id_type=pl.DeviceIdType.MESH
+            )
+
+    def send(k):
+        row, col, there = partner(k, -1)
+        copy = pltpu.make_async_remote_copy(
+            src_ref=picked.at[k],
+            dst_ref=arrived.at[k],
+            send_sem=out_sem.at[k],
+            recv_sem=in_sem.at[k],
+            device_id=(row, col),
+            device_id_type=pl.DeviceIdType.MESH,
+        )
+        return copy, there
+
+    def send_back(k):
+        row, col, there = partner(k, 1)
+        copy = pltpu.make_async_remote_copy(
+            src_ref=weighted.at[k],
+            dst_ref=returned.at[k],
+            send_sem=back_out_sem.at[k],
+            recv_sem=back_in_sem.at[k],
+            device_id=(row, col),
+            device_id_type=pl.DeviceIdType.MESH,
+        )
+        return copy, there
+
+    sublane, gather, scatter, span, fill = helpers(rows)
+
     for load in loads[:5]:
         load.wait()
     gsea = response_ref[...] * mask_ref[...].astype(F32)
@@ -252,10 +264,6 @@
         load.wait()
 
     group = min(rows, 64)
-
-    def at_level(k, base):
-        first = (k // SUB) * rows * SUB + (k % SUB)
-        return pl.ds(first + base * SUB, group, stride=SUB)
 
     @pl.loop(0, rows // group)
     def _(b):
@@ -263,17 +271,24 @@
         e = jnp.zeros((group, LANES), F32)
         g = jnp.zeros((group, LANES), F32)
         for k in range(levels - 1, -1, -1):
-            low = lower[at_level(k, base), :]
-            up = upper[at_level(k, base), :]
-            rhs = temp[at_level(k, base), :]
+            low = lower[at_level(k, base, rows, group), :]
+            up = upper[at_level(k, base, rows, group), :]
+            rhs = temp[at_level(k, base, rows, group), :]
             inverse = 1.0 / (1.0 + low + up - up * g)
             e = (rhs + up * e) * inverse
             g = low * inverse
             e_all[k, pl.ds(base, group), :] = e
-            if k:
-                g_all[k, pl.ds(base, group), :] = g
+            g_all[k, pl.ds(base, group), :] = g
         f_low[pl.ds(base, group), :] = inverse
 
+    stores = [
+        pltpu.make_async_copy(source, dest, store_sem.at[n])
+        for n, (source, dest) in enumerate(
+            ((e_all, e_hbm), (g_all, g_hbm), (bottom, bottom_hbm))
+        )
+    ]
+    stores[0].start()
+    stores[1].start()
     fill(atm_table, e_all[0], f_low[...])
     atm_sum[...] = jnp.zeros_like(atm_sum)
 
@@ -311,59 +326,106 @@
         def _():
             copy.start()
 
-    returned[LOCAL] = weighted[LOCAL]
+    own = pltpu.make_async_copy(weighted.at[LOCAL], returned.at[LOCAL], own_sem)
+    own.start()
+    flux = (atm_sum[:, :LANES] + atm_sum[:, LANES:]) / atm_area_ref[...]
+    bottom[...] = e_all[0] + f_low[...] * flux
+    stores[2].start()
+
+    @pl.loop(0, offsets)
+    def _(k):
+        back, _ = send_back(k)
+        _, _, there = partner(k, -1)
+
+        @pl.when(there & (k != LOCAL))
+        def _():
+            back.wait_recv()
+
+    @pl.loop(0, offsets)
+    def _(k):
+        forth, there = send(k)
+
+        @pl.when(there & (k != LOCAL))
+        def _():
+            forth.wait_send()
+
+        back, there = send_back(k)
+
+        @pl.when(there & (k != LOCAL))
+        def _():
+            back.wait_send()
+
+    own.wait()
+    for store in stores:
+        store.wait()
+
+
+def finish(n_lat, n_lon, *refs):
+    sources, (level_hbm, fresh_hbm), refs = refs[:10], refs[10:12], refs[12:]
+    (
+        ocean_ref,
+        returned,
+        surface_ref,
+        warming_ref,
+        response_ref,
+        mask_ref,
+        ocean_area_ref,
+        bottom,
+        e_all,
+        g_all,
+    ) = refs[:10]
+    level, fresh, ocean_sum, load_sem, store_sem = refs[10:]
+    loads = [
+        pltpu.make_async_copy(source, dest, load_sem.at[n])
+        for n, (source, dest) in enumerate(zip(sources, refs[:10]))
+    ]
+    for load in loads:
+        load.start()
+    offsets, blocks, _ = ocean_ref.shape
+    levels, rows, _ = e_all.shape
+    _, _, scatter, span, _ = helpers(rows)
+    ocean_sum[...] = jnp.zeros_like(ocean_sum)
+    loads[0].wait()
+    loads[1].wait()
+
+    def add_up(first, last):
+        @pl.loop(first, last)
+        def _(k):
+            _, _, there = partner_of(n_lat, n_lon, k, -1)
+
+            @pl.when(there)
+            def _():
+                total = ocean_sum[...]
+                for n in range(blocks // SUB):
+                    total = total + scatter(ocean_ref[k, span(n), :], returned[k, span(n), :])
+                ocean_sum[...] = total
+
+    add_up(0, offsets // 2)
+    for load in loads[2:]:
+        load.wait()
+
+    group = min(rows, 64)
 
     @pl.loop(0, rows // group)
     def _(b):
         base = pl.multiple_of(b * group, group)
         here = pl.ds(base, group)
-        flux = (atm_sum[here, :LANES] + atm_sum[here, LANES:]) / atm_area_ref[here, :]
-        value = e_all[0, here, :] + f_low[here, :] * flux
-        level[at_level(0, base), :] = value
+        value = bottom[here, :]
+        level[at_level(0, base, rows, group), :] = value
         for k in range(1, levels):
             value = e_all[k, here, :] + g_all[k, here, :] * value
-            level[at_level(k, base), :] = value
-
-    store = pltpu.make_async_copy(level, level_hbm, store_sem)
+            level[at_level(k, base, rows, group), :] = value
+
+    store = pltpu.make_async_copy(level, level_hbm, store_sem.at[0])
     store.start()
-    ocean_sum[...] = jnp.zeros_like(ocean_sum)
-
-    @pl.loop(0, offsets)
-    def _(t):
-        k = order(t)
-        _, _, there = partner(k, -1)
-        incoming, _ = send_back(k)
-
-        @pl.when(there & (k != LOCAL))
-        def _():
-            incoming.wait_recv()
-
-        @pl.when(there)
-        def _():
-            total = ocean_sum[...]
-            for n in range(pieces):
-                total = total + scatter(ocean_ref[k, span(n), :], returned[k, span(n), :])
-            ocean_sum[...] = total
-
+    add_up(offsets // 2, offsets)
     ocean_flux = (ocean_sum[:, :LANES] + ocean_sum[:, LANES:]) / ocean_area_ref[...]
     gsea = response_ref[...] * mask_ref[...].astype(F32)
-    fresh_ref[...] = surface_ref[...] + gsea * (warming_ref[...] - ocean_flux)
-
-    @pl.loop(0, offsets)
-    def _(k):
-        forth, there = send(k)
-
-        @pl.when(there & (k != LOCAL))
-        def _():
-            forth.wait_send()
-
-        back, there = send_back(k)
-
-        @pl.when(there & (k != LOCAL))
-        def _():
-            back.wait_send()
-
+    fresh[...] = surface_ref[...] + gsea * (warming_ref[...] - ocean_flux)
+    last = pltpu.make_async_copy(fresh, fresh_hbm, store_sem.at[1])
+    last.start()
     store.wait()
+    last.wait()
 
 
 def on_device(
@@ -398,44 +460,40 @@
     def cells(array):
         return array.reshape(offsets, slots // LANES, LANES)
 
-    operands = [cells(cell_ocean)]
-    operands += [square(a) for a in (surface_temp, extra_warming, response, sea_mask)]
+    ocean = [square(a) for a in (surface_temp, extra_warming, response, sea_mask)]
+    operands = [cells(cell_ocean)] + ocean
+    operands += [tiles(a) for a in (lower, upper, old_temp)]
     operands += [cells(a) for a in (cell_column, exchange_cell_weight, cell_coef)]
-    operands += [square(a) for a in (atm_area, ocean_area)]
-    operands += [tiles(a) for a in (lower, upper, old_temp)]
-    vmem = pl.BlockSpec(memory_space=pltpu.VMEM)
+    operands += [square(atm_area)]
     smem = pl.BlockSpec(memory_space=pltpu.SMEM)
     hbm = pl.BlockSpec(memory_space=pl.ANY)
-    flat = pltpu.VMEM((levels * rows, LANES), F32)
-    deep = pltpu.VMEM((levels, rows, LANES), F32)
+    plane = (rows, LANES)
+    deep = (levels, rows, LANES)
+    fluxes = (offsets, slots // LANES, LANES)
     table = pltpu.VMEM((2 * rows, 2 * LANES), BF16)
     states = pltpu.VMEM((offsets, 2, slots // LANES, LANES), F32)
-    fluxes = pltpu.VMEM((offsets, slots // LANES, LANES), F32)
     total = pltpu.VMEM((rows, 2 * LANES), F32)
     sem = pltpu.SemaphoreType.DMA((offsets,))
-    level, fresh = pl.pallas_call(
+    limit = 60 * 1024 * 1024
+    e_all, g_all, bottom, returned = pl.pallas_call(
         functools.partial(kernel, n_lat, n_lon),
-        out_shape=(
-            jax.ShapeDtypeStruct((levels * rows, LANES), F32),
-            jax.ShapeDtypeStruct((rows, LANES), F32),
-        ),
+        out_shape=[jax.ShapeDtypeStruct(shape, F32) for shape in (deep, deep, plane, fluxes)],
         in_specs=[smem] + [hbm] * len(operands),
-        out_specs=(hbm, vmem),
+        out_specs=[hbm] * 4,
         scratch_shapes=[pltpu.VMEM(a.shape, a.dtype) for a in operands]
         + [
-            deep,
-            deep,
-            flat,
+            pltpu.VMEM(deep, F32),
+            pltpu.VMEM(deep, F32),
+            pltpu.VMEM(plane, F32),
             table,
             table,
-            pltpu.VMEM((rows, LANES), F32),
+            pltpu.VMEM(plane, F32),
             states,
             states,
-            fluxes,
-            fluxes,
-            total,
+            pltpu.VMEM(fluxes, F32),
             total,
             pltpu.SemaphoreType.DMA((len(operands),)),
+            pltpu.SemaphoreType.DMA((3,)),
             pltpu.SemaphoreType.DMA,
             sem,
             sem,
@@ -443,9 +501,26 @@
             sem,
         ],
         compiler_params=pltpu.CompilerParams(
-            collective_id=0, has_side_effects=True, vmem_limit_bytes=60 * 1024 * 1024
+            collective_id=0, has_side_effects=True, vmem_limit_bytes=limit
         ),
     )(pair_count, *operands)
+    operands = [cells(cell_ocean), returned] + ocean + [square(ocean_area), bottom, e_all, g_all]
+    flat = (levels * rows, LANES)
+    level, fresh = pl.pallas_call(
+        functools.partial(finish, n_lat, n_lon),
+        out_shape=[jax.ShapeDtypeStruct(shape, F32) for shape in (flat, plane)],
+        in_specs=[hbm] * len(operands),
+        out_specs=[hbm] * 2,
+        scratch_shapes=[pltpu.VMEM(a.shape, a.dtype) for a in operands]
+        + [
+            pltpu.VMEM(flat, F32),
+            pltpu.VMEM(plane, F32),
+            total,
+            pltpu.SemaphoreType.DMA((len(operands),)),
+            pltpu.SemaphoreType.DMA((2,)),
+        ],
+        compiler_params=pltpu.CompilerParams(vmem_limit_bytes=limit),
+    )(*operands)
     level = level.reshape(levels // SUB, rows, SUB, LANES).transpose(0, 2, 1, 3)
     return level.reshape(levels, ncols), fresh.reshape(-1)
 

time: 46.7 us -> 44.3 us (0.949)
  local copies, waits for them, and re-layouts: 3.72 us -> 0 us
  Pallas kernels: 42.2 us -> 43.5 us
    unnamed x4 -> x0, local copies, waits for them, and re-layouts: 3.72 us -> none
    pallas_call x1 -> x2, Pallas kernels: 42.2 us -> 43.5 us  [the longest x1 33.7 us: on_device(): pl.pallas_call(functools.partial(kernel, n_lat, n_lon), out_shape=[jax.Sh...]
where the time goes in v1:
time: 44.3 us; the launch traced here: 44.2 us
  Pallas kernels  43.5 us (98%)
  between operations  0.64 us (1%)
    pallas_call x1, Pallas kernels, on_device(): pl.pallas_call(functools.partial(kernel, n_lat, n_lon), out_shape=[jax.Sh...  33.7 us
    pallas_call x1, Pallas kernels, on_device(): pl.pallas_call(functools.partial(finish, n_lat, n_lon), out_shape=[jax.Sh...  9.83 us

profile of v1, /device:TPU:1, one launch (start us, length us, event | category | flops | bytes accessed | tf_op | source)
XLA Modules:
  0.0 44.2 jit_solution(8805191555173951460)
XLA Ops:
  0.6 33.7 %shard_map.149 = (f32[32,128,128]{2,1,0:T(8,128)}, f32[32,128,128]{2,1,0:T(8,128)}, f32[128,128]{1,0:T(8,128)}, f32[10,32,128]{2,1,0:T(8,128)}) custom-call(s32[1,10]{1,0:T(1,128)} %count_ref.1, s32[10,32,128]{2,1,0:T(8,128)} %bitcast.34, f32[128,128]{1,0:T(8,128)} %bitcast.36, f32[128,128]{1,0:T(8,128)} %bitcast.38, f32[128,128]{1,0:T(8,128)} %bitcast.40, ...), custom_call_target="tpu_custom_call" | custom-call | tf_op jit(solution)/shard_map/pallas_call | solution.py:478
  34.4 9.8 %shard_map.150 = (f32[4096,128]{1,0:T(8,128)}, f32[128,128]{1,0:T(8,128)}) custom-call(s32[10,32,128]{2,1,0:T(8,128)} %bitcast.35, f32[10,32,128]{2,1,0:T(8,128)} %get-tuple-element.8.refs_1_, f32[128,128]{1,0:T(8,128)} %bitcast.37, f32[128,128]{1,0:T(8,128)} %bitcast.39, f32[128,128]{1,0:T(8,128)} %bitcast.41, s32[128,128]{1,0:T(8,128)} %bitcast.43, ...), custom_call_target="tpu_custom_call" | custom-call | tf_op jit(solution)/shard_map/pallas_call | solution.py:509
